TPU v7x, 256 devices: a whole 4x4x8 slice. The times are simulated.
256 devices in a mesh: row: 32 (over y, z_hi, core), col: 8 (over z_lo, x).
Axes of the slice: x: 4, y: 4, z: 8 (z_hi: 4, z_lo: 2; z = z_hi * 2 + z_lo), core: 2. Of those that a mesh axis runs over, the one named last changes fastest.
Arguments:
- grad_out: bfloat16 [4096, 16384], P('col', 'row'), may hold values from -6 to 6
- inputs: bfloat16 [4096, 16384], P('col', 'row'), may hold values from -6 to 6
- gate_pre: bfloat16 [4096, 4096], P('row', 'col'), may hold values from -8 to 8
- up_pre: bfloat16 [4096, 4096], P('row', 'col'), may hold values from -6 to 6
- w_gate: bfloat16 [16384, 4096], P('row', 'col'), may hold values from -0.046875 to 0.046875
- w_up: bfloat16 [16384, 4096], P('row', 'col'), may hold values from -0.046875 to 0.046875
- w_down: bfloat16 [4096, 16384], P('col', 'row'), may hold values from -0.046875 to 0.046875
Outputs:
- input_grad: bfloat16 [4096, 16384], P('col', 'row')
- gate_grad: bfloat16 [16384, 4096], P('row', 'col')
- up_grad: bfloat16 [16384, 4096], P('row', 'col')
- down_grad: bfloat16 [4096, 16384], P('col', 'row')
All inputs are finite; a program needn't handle non-finite values.
Results may differ from a plain program's by a relative error of at most 0.0049.
Values may be sent and summed in bfloat16 or wider, within the bound.
A program may use at most 128 MiB of HBM per device.

v0:
```python
import jax
import jax.numpy as jnp
from jax import lax
from jax.sharding import PartitionSpec as P


def times_transposed(left, right):
    return lax.dot_general(
        left, right, (((1,), (1,)), ((), ())), preferred_element_type=jnp.float32
    )


def over_tokens(left, right):
    return lax.dot_general(
        left, right, (((0,), (0,)), ((), ())), preferred_element_type=jnp.float32
    )


def local_grads(grad_hidden, gate_pre, up_pre):
    gate_val = gate_pre.astype(jnp.float32)
    up_val = up_pre.astype(jnp.float32)
    sig_gate = jax.nn.sigmoid(gate_val)
    act_gate = gate_val * sig_gate
    hidden = (act_gate * up_val).astype(jnp.bfloat16)
    grad_gate = (grad_hidden * up_val * sig_gate * (1.0 + gate_val * (1.0 - sig_gate))).astype(
        jnp.bfloat16
    )
    grad_up = (grad_hidden * act_gate).astype(jnp.bfloat16)
    return (hidden, grad_gate, grad_up)


def per_device(grad_out, inputs, gate_pre, up_pre, w_gate, w_up, w_down):
    grad_rows, input_rows = (
        lax.all_gather(grad_out, "col", axis=0, tiled=True),
        lax.all_gather(inputs, "col", axis=0, tiled=True),
    )
    grad_hidden = lax.psum_scatter(
        times_transposed(grad_rows, w_down), "row", scatter_dimension=0, tiled=True
    )
    own_hidden, own_gate, own_up = local_grads(grad_hidden, gate_pre, up_pre)
    hidden, grad_gate, grad_up = (
        lax.all_gather(own_hidden, "row", axis=0, tiled=True),
        lax.all_gather(own_gate, "row", axis=0, tiled=True),
        lax.all_gather(own_up, "row", axis=0, tiled=True),
    )
    grad_scale = grad_rows.shape[0] ** (-0.5)
    down_grad = (over_tokens(hidden, grad_rows) * grad_scale).astype(jnp.bfloat16)
    gate_grad = (over_tokens(input_rows, grad_gate) * grad_scale).astype(jnp.bfloat16)
    up_grad = (over_tokens(input_rows, grad_up) * grad_scale).astype(jnp.bfloat16)
    input_grad = lax.psum_scatter(
        times_transposed(grad_gate, w_gate) + times_transposed(grad_up, w_up),
        "col",
        scatter_dimension=0,
        tiled=True,
    ).astype(jnp.bfloat16)
    return (input_grad, gate_grad, up_grad, down_grad)


def solution(mesh):
    placed = (
        P("col", "row"),
        P("col", "row"),
        P("row", "col"),
        P("row", "col"),
        P("row", "col"),
        P("row", "col"),
        P("col", "row"),
    )
    return jax.shard_map(
        per_device,
        mesh=mesh,
        in_specs=placed,
        out_specs=(P("col", "row"), P("row", "col"), P("row", "col"), P("col", "row")),
        check_vma=False,
    )
```

profile of v0, /device:TPU:1, one launch (start us, length us, event | category | flops | bytes accessed | tf_op | source)
XLA Modules:
  0.0 541.1 jit_solution(10941688823285014997)
XLA Ops:
  7.2 0.0 copy-start
  7.2 0.0 all-gather.6.cloned.1.call-start
  7.2 0.7 all-gather.6.cloned.1.call-update
  7.9 0.0 reduce-scatter.3.cloned.1.call-start
  8.0 60.9 %all-gather.6.cloned.1.call-done = bf16[4096,512]{1,0:T(8,128)(2,1)} async-done(((bf16[512,512]{1,0:T(8,128)(2,1)}), bf16[4096,512]{1,0:T(8,128)(2,1)}) %all-gather.6.cloned.1.call-update) | async-done | bytes 4194320 | tf_op jit(solution)/shard_map/all_gather | solution.py:34
  68.8 0.0 copy-done
  68.8 7.8 %fusion.13 = f32[4096,512]{1,0:T(8,128)} fusion(bf16[4096,512]{1,0:T(8,128)(2,1)} %all-gather.6.cloned.1.call-done, bf16[512,512]{1,0:T(8,128)(2,1)S(1)} %copy-done), kind=kOutput, calls=%fused_computation.23 | convolution fusion | flops 2147483648 | bytes 13107200 | tf_op jit(solution)/shard_map/dot_general | solution.py:8
  76.6 0.0 copy-start.3
  76.6 0.0 copy-start.4
  76.6 0.0 copy-start.1
  76.6 0.0 reduce-scatter.3.cloned.1.call-update
  76.7 0.0 all-gather.8.cloned.1.call-start
  76.7 119.6 %reduce-scatter.3.cloned.1.call-done = f32[128,512]{1,0:T(8,128)} async-done(((f32[4096,512]{1,0:T(8,128)}), f32[128,512]{1,0:T(8,128)}) %reduce-scatter.3.cloned.1.call-update) | async-done | bytes 262160 | tf_op jit(solution)/shard_map/reduce_scatter | solution.py:37
  196.3 0.0 copy-done.3
  196.3 0.0 copy-done.4
  196.4 1.8 multiply_convert_fusion
  198.2 0.0 all-gather.8.cloned.1.call-update
  198.2 0.0 all-gather.10.cloned.1.call-start
  198.3 0.5 all-gather.10.cloned.1.call-update
  198.8 0.0 all-gather.12.cloned.1.call-start
  198.8 0.5 all-gather.12.cloned.1.call-update
  199.4 0.0 all-gather.14.cloned.1.call-start
  199.4 0.5 all-gather.14.cloned.1.call-update
  199.9 0.0 copy-start.2
  200.0 0.2 reduce-scatter.5.cloned.1.call-start
  200.2 58.6 %all-gather.8.cloned.1.call-done = bf16[4096,512]{1,0:T(8,128)(2,1)} async-done(((bf16[128,512]{1,0:T(8,128)(2,1)}), bf16[4096,512]{1,0:T(8,128)(2,1)}) %all-gather.8.cloned.1.call-update) | async-done | bytes 4194320 | tf_op jit(solution)/shard_map/all_gather | solution.py:43
  258.8 0.0 copy-done.1
  258.8 7.8 %fusion.14 = f32[4096,512]{1,0:T(8,128)} fusion(bf16[4096,512]{1,0:T(8,128)(2,1)} %all-gather.8.cloned.1.call-done, bf16[512,512]{1,0:T(8,128)(2,1)S(1)} %copy-done.1), kind=kOutput, calls=%fused_computation.24 | convolution fusion | flops 2147483648 | bytes 13107200 | tf_op jit(solution)/shard_map/dot_general | solution.py:8
  266.6 53.5 %all-gather.10.cloned.1.call-done = bf16[4096,512]{1,0:T(8,128)(2,1)} async-done(((bf16[128,512]{1,0:T(8,128)(2,1)}), bf16[4096,512]{1,0:T(8,128)(2,1)}) %all-gather.10.cloned.1.call-update) | async-done | bytes 4194320 | tf_op jit(solution)/shard_map/all_gather | solution.py:44
  320.0 0.0 copy-done.2
  320.0 10.3 %convolution_add_fusion = f32[4096,512]{1,0:T(8,128)} fusion(f32[4096,512]{1,0:T(8,128)} %fusion.14, bf16[4096,512]{1,0:T(8,128)(2,1)} %all-gather.10.cloned.1.call-done, bf16[512,512]{1,0:T(8,128)(2,1)S(1)} %copy-done.2), kind=kOutput, calls=%fused_computation | convolution fusion | flops 2149580800 | bytes 21495808 | tf_op jit(solution)/shard_map/dot_general | solution.py:8
  330.3 0.0 reduce-scatter.5.cloned.1.call-update
  330.3 43.7 %all-gather.12.cloned.1.call-done = bf16[4096,512]{1,0:T(8,128)(2,1)} async-done(((bf16[512,512]{1,0:T(8,128)(2,1)}), bf16[4096,512]{1,0:T(8,128)(2,1)}) %all-gather.12.cloned.1.call-update) | async-done | bytes 4194320 | tf_op jit(solution)/shard_map/all_gather | solution.py:35
  374.1 5.8 %fusion.3 = bf16[512,512]{0,1:T(8,128)(2,1)S(1)} fusion(bf16[4096,512]{1,0:T(8,128)(2,1)} %all-gather.10.cloned.1.call-done, bf16[4096,512]{1,0:T(8,128)(2,1)} %all-gather.12.cloned.1.call-done), kind=kOutput, calls=%fused_computation.7 | convolution fusion | flops 2148007936 | bytes 8912896 | tf_op jit(solution)/shard_map/dot_general | solution.py:14
  379.9 1.0 copy.12
  380.9 5.8 %fusion.4 = bf16[512,512]{0,1:T(8,128)(2,1)S(1)} fusion(bf16[4096,512]{1,0:T(8,128)(2,1)} %all-gather.8.cloned.1.call-done, bf16[4096,512]{1,0:T(8,128)(2,1)} %all-gather.12.cloned.1.call-done), kind=kOutput, calls=%fused_computation.8 | convolution fusion | flops 2148007936 | bytes 8912896 | tf_op jit(solution)/shard_map/dot_general | solution.py:14
  386.7 1.0 copy.11
  387.7 49.4 %all-gather.14.cloned.1.call-done = bf16[4096,512]{1,0:T(8,128)(2,1)} async-done(((bf16[128,512]{1,0:T(8,128)(2,1)}), bf16[4096,512]{1,0:T(8,128)(2,1)}) %all-gather.14.cloned.1.call-update) | async-done | bytes 4194320 | tf_op jit(solution)/shard_map/all_gather | solution.py:42
  437.1 6.6 %fusion.2 = bf16[512,512]{1,0:T(8,128)(2,1)} fusion(bf16[4096,512]{1,0:T(8,128)(2,1)} %all-gather.14.cloned.1.call-done, bf16[4096,512]{1,0:T(8,128)(2,1)} %all-gather.6.cloned.1.call-done), kind=kOutput, calls=%fused_computation.6 | convolution fusion | flops 2148007936 | bytes 8912896 | tf_op jit(solution)/shard_map/dot_general | solution.py:14
  443.7 88.5 %reduce-scatter.5.cloned.1.call-done = f32[512,512]{1,0:T(8,128)} async-done(((f32[4096,512]{1,0:T(8,128)}), f32[512,512]{1,0:T(8,128)}) %reduce-scatter.5.cloned.1.call-update) | async-done | bytes 1048592 | tf_op jit(solution)/shard_map/reduce_scatter | solution.py:50
  532.2 2.1 convert_element_type.37
Async XLA Ops:
  7.2 61.7 %copy-start = (bf16[512,512]{1,0:T(8,128)(2,1)S(1)}, bf16[512,512]{1,0:T(8,128)(2,1)}, u32[]{:S(2)}) copy-start(bf16[512,512]{1,0:T(8,128)(2,1)} %param.13) | copy-start | bytes 1572868
  7.2 61.6 %all-gather.6.cloned.1.call-start = ((), (), s32[]{:S(2)}) async-start(), calls=%async_computation.2 | async-start | bytes 4718592 | tf_op jit(solution)/shard_map/all_gather | solution.py:34
  7.9 188.4 %reduce-scatter.3.cloned.1.call-start = ((), (), s32[]{:S(2)}) async-start(), calls=%async_computation.3 | async-start | bytes 8650752 | tf_op jit(solution)/shard_map/reduce_scatter | solution.py:37
  76.6 119.7 %copy-start.3 = (bf16[128,512]{1,0:T(8,128)(2,1)S(1)}, bf16[128,512]{1,0:T(8,128)(2,1)}, u32[]{:S(2)}) copy-start(bf16[128,512]{1,0:T(8,128)(2,1)} %param.9) | copy-start | bytes 393220
  76.6 119.7 %copy-start.4 = (bf16[128,512]{1,0:T(8,128)(2,1)S(1)}, bf16[128,512]{1,0:T(8,128)(2,1)}, u32[]{:S(2)}) copy-start(bf16[128,512]{1,0:T(8,128)(2,1)} %param.10) | copy-start | bytes 393220
  76.6 182.1 %copy-start.1 = (bf16[512,512]{1,0:T(8,128)(2,1)S(1)}, bf16[512,512]{1,0:T(8,128)(2,1)}, u32[]{:S(2)}) copy-start(bf16[512,512]{1,0:T(8,128)(2,1)} %param.11) | copy-start | bytes 1572868
  76.7 182.1 %all-gather.8.cloned.1.call-start = ((), (), s32[]{:S(2)}) async-start(), calls=%async_computation.4 | async-start | bytes 4325376 | tf_op jit(solution)/shard_map/all_gather | solution.py:43
  198.2 121.8 %all-gather.10.cloned.1.call-start = ((), (), s32[]{:S(2)}) async-start(), calls=%async_computation.5 | async-start | bytes 4325376 | tf_op jit(solution)/shard_map/all_gather | solution.py:44
  198.8 175.3 %all-gather.12.cloned.1.call-start = ((), (), s32[]{:S(2)}) async-start(), calls=%async_computation.7 | async-start | bytes 4718592 | tf_op jit(solution)/shard_map/all_gather | solution.py:35
  199.4 237.7 %all-gather.14.cloned.1.call-start = ((), (), s32[]{:S(2)}) async-start(), calls=%async_computation.8 | async-start | bytes 4325376 | tf_op jit(solution)/shard_map/all_gather | solution.py:42
  199.9 120.1 %copy-start.2 = (bf16[512,512]{1,0:T(8,128)(2,1)S(1)}, bf16[512,512]{1,0:T(8,128)(2,1)}, u32[]{:S(2)}) copy-start(bf16[512,512]{1,0:T(8,128)(2,1)} %param.12) | copy-start | bytes 1572868
  200.0 332.3 %reduce-scatter.5.cloned.1.call-start = ((), (), s32[]{:S(2)}) async-start(), calls=%async_computation.6 | async-start | bytes 9437184 | tf_op jit(solution)/shard_map/reduce_scatter | solution.py:50
Sparse Core Ops, SparseCore 0:
  9.8 58.9 all-gather.5
  76.8 119.5 reduce-scatter.2
  199.8 58.9 all-gather.7
  262.1 57.9 all-gather.9
  321.8 52.2 all-gather.11
  377.4 59.6 all-gather.13
  439.8 92.3 reduce-scatter.4
where the time goes:
time: 541 us
  waiting for transfers between devices  476 us (88%)
  matrix products  44.1 us (8%)
  between operations  14.2 us (3%)
    reduce_scatter x1, waiting for transfers between devices, per_device(): lax.psum_scatter(times_transposed(grad_rows, w_down), 'row', scatter_dime...  120 us
    reduce_scatter x1, waiting for transfers between devices, per_device(): lax.psum_scatter(times_transposed(grad_gate, w_gate) + times_transposed(g...  88.5 us
    all_gather x1, waiting for transfers between devices, per_device(): lax.all_gather(grad_out, 'col', axis=0, tiled=True)  60.9 us
    all_gather x1, waiting for transfers between devices, per_device(): lax.all_gather(own_gate, 'row', axis=0, tiled=True)  58.6 us
    all_gather x1, waiting for transfers between devices, per_device(): lax.all_gather(own_up, 'row', axis=0, tiled=True)  53.5 us
    all_gather x1, waiting for transfers between devices, per_device(): lax.all_gather(own_hidden, 'row', axis=0, tiled=True)  49.4 us
    all_gather x1, waiting for transfers between devices, per_device(): lax.all_gather(inputs, 'col', axis=0, tiled=True)  43.7 us
    dot_general x3, matrix products, times_transposed(): lax.dot_general(left, right, (((1,), (1,)), ((), ())), preferred_element_...  25.9 us
  transfers between devices with their start and end apart: 7, of which 7 were waited for; matrix products, arithmetic and copies ran while one was open for 7% of the time, Pallas kernels for 0%

commit v1 on v0

v1 whole, which is shorter than its diff:
```python
import functools

import jax
import jax.numpy as jnp
from jax import lax
from jax.experimental import pallas as pl
from jax.experimental.pallas import tpu as pltpu
from jax.sharding import PartitionSpec as P

MESH = pl.DeviceIdType.MESH
F32, BF16 = jnp.float32, jnp.bfloat16
B = 512
ROWS = 128
ORDER = ((0, 0), (1, 0), (0, 1), (0, 3), (0, 2), (1, 1), (1, 3), (1, 2))
AT = {where: place for place, where in enumerate(ORDER)}
NT = (((1,), (1,)), ((), ()))
TN = (((0,), (0,)), ((), ()))


def kernel(
    go_ref, in_ref, gate_ref, up_ref, wg_ref, wu_ref, wd_ref,
    ig_ref, gg_ref, ug_ref, dg_ref,
    go, inp, act, gh, part, own, core_in,
    y_out, y_mid, y_in, h_sum, h_in, x_out, x_in, acc,
    send_sem, recv_sem,
):
    row, col = lax.axis_index("row"), lax.axis_index("col")
    k, h, y = lax.rem(row, 2), lax.rem(row // 2, 4), row // 8
    x, z = lax.rem(col, 4), col // 4

    def up_to(v, n):
        return lax.rem(v, n)

    def row_of(y_, h_, k_):
        return (y_ * 4 + h_) * 2 + k_

    x_right, x_left, x_far = ((row, z * 4 + up_to(x + d, 4)) for d in (1, 3, 2))
    z_pair = (row, (1 - z) * 4 + x)
    y_next, y_prev, y_far = (up_to(y + d, 4) for d in (1, 3, 2))
    y_right, y_left = ((row_of(v, h, k), col) for v in (y_next, y_prev))
    h_next, h_prev, h_far = (up_to(h + d, 4) for d in (1, 3, 2))
    h_right, h_left, h_over = ((row_of(y, v, k), col) for v in (h_next, h_prev, h_far))
    twin = (row_of(y, h, 1 - k), col)
    friends = (x_right, x_left, x_far, z_pair, y_right, y_left, h_right, h_left, h_over, twin)

    barrier = pltpu.get_barrier_semaphore()
    for friend in friends:
        pl.semaphore_signal(barrier, inc=1, device_id=friend, device_id_type=MESH)
    pl.semaphore_wait(barrier, len(friends))

    copies = []

    def send(src, dst, to):
        n = len(copies)
        copy = pltpu.make_async_remote_copy(
            src_ref=src, dst_ref=dst, send_sem=send_sem.at[n], recv_sem=recv_sem.at[n],
            device_id=to, device_id_type=MESH,
        )
        copy.start()
        copies.append([copy, False])
        return n

    def arrived(*ns):
        for n in ns:
            copies[n][0].wait_recv()

    def gone(*ns):
        for n in ns:
            if not copies[n][1]:
                copies[n][0].wait_send()
                copies[n][1] = True

    first, second = pl.ds(0, B // 2), pl.ds(B // 2, B // 2)

    def gather_own(src, buf):
        return (
            send(src, buf.at[AT[0, 3]], x_right),
            send(src, buf.at[AT[0, 1]], x_left),
            send(src, buf.at[AT[1, 0]], z_pair),
        )

    def gather_pair(buf):
        return (
            send(buf.at[AT[1, 0]], buf.at[AT[1, 3]], x_right),
            send(buf.at[AT[1, 0]], buf.at[AT[1, 1]], x_left),
        )

    def gather_far(buf, plane):
        return (
            send(buf.at[AT[plane, 3], first], buf.at[AT[plane, 2], first], x_right),
            send(buf.at[AT[plane, 1], second], buf.at[AT[plane, 2], second], x_left),
        )

    def product(g, half, to):
        @pl.loop(0, 4)
        def _(i):
            place = g * 4 + half * 2 + i // 2
            tile = go[place, pl.ds(pl.multiple_of(lax.rem(i, 2) * 256, 256), 256)]
            to[g, pl.ds(pl.multiple_of(i * 256, 256), 256)] = lax.dot_general(
                tile, wd_ref[...], NT, preferred_element_type=F32
            )

    def products(g):
        product(g, 1 - k, part)
        n = send(part.at[g], core_in.at[g], twin)
        product(g, k, own)
        return n

    def pair_sum(g, v, lo, n):
        rows = pl.ds(pl.multiple_of(v * 256 + lo, 128), n)
        return own[g, rows] + core_in[g, rows]

    lo, hi = pl.ds(0, 128), pl.ds(128, 128)

    def y_first(g):
        y_out[g, 0] = pair_sum(g, y_far, 0, 256).astype(BF16)
        a = send(y_out.at[g, 0, lo], y_mid.at[g, 0], y_right)
        b = send(y_out.at[g, 0, hi], y_mid.at[g, 1], y_left)
        y_out[g, 1, hi] = pair_sum(g, y_next, 128, 128).astype(BF16)
        c = send(y_out.at[g, 1, hi], y_in.at[g, 0, hi], y_right)
        y_out[g, 2, lo] = pair_sum(g, y_prev, 0, 128).astype(BF16)
        d = send(y_out.at[g, 2, lo], y_in.at[g, 1, lo], y_left)
        return a, b, c, d

    def y_second(g, ns):
        arrived(ns[0])
        y_out[g, 1, lo] = (pair_sum(g, y_next, 0, 128) + y_mid[g, 0].astype(F32)).astype(BF16)
        a = send(y_out.at[g, 1, lo], y_in.at[g, 0, lo], y_right)
        arrived(ns[1])
        y_out[g, 2, hi] = (pair_sum(g, y_prev, 128, 128) + y_mid[g, 1].astype(F32)).astype(BF16)
        b = send(y_out.at[g, 2, hi], y_in.at[g, 1, hi], y_left)
        return a, b

    def h_first(g, ns):
        arrived(*ns)
        h_sum[g] = pair_sum(g, y, 0, 256) + y_in[g, 0].astype(F32) + y_in[g, 1].astype(F32)

        def at(v):
            return h_sum.at[g, pl.ds(pl.multiple_of(v * 64, 64), 64)]

        return (
            send(at(h_far), h_in.at[g, 2], h_over),
            send(at(h_next), h_in.at[g, 0], h_right),
            send(at(h_prev), h_in.at[g, 1], h_left),
        )

    def gh_rows(g, y_, at_, n):
        return gh.at[pl.ds(pl.multiple_of(g * 2048 + k * 1024 + y_ * 256 + at_, 64), n)]

    def h_last(g, ns):
        arrived(*ns)
        mine = pl.ds(pl.multiple_of(h * 64, 64), 64)
        total = h_sum[g, mine] + h_in[g, 0] + h_in[g, 1] + h_in[g, 2]
        ref = gh_rows(g, y, h * 64, 64)
        ref[...] = total.astype(BF16)
        return tuple(send(ref, ref, to) for to in (h_over, h_right, h_left))

    def y_gather(g, ns):
        arrived(*ns)
        ref = gh_rows(g, y, 0, 256)
        return tuple(send(ref, ref, to) for to in (y_right, y_left, twin))

    def y_forward(g, ns):
        arrived(ns[0])
        ref = gh_rows(g, y_prev, 0, 128)
        a = send(ref, ref, y_right)
        ref = gh_rows(g, y_prev, 0, 256)
        b = send(ref, ref, twin)
        arrived(ns[1])
        ref = gh_rows(g, y_next, 128, 128)
        c = send(ref, ref, y_left)
        ref = gh_rows(g, y_next, 0, 256)
        d = send(ref, ref, twin)
        return a, b, c, d

    def y_last(g, ns):
        arrived(ns[0], ns[2])
        ref = gh_rows(g, y_far, 0, 256)
        return send(ref, ref, twin)

    def act_rows(v):
        return pl.ds(pl.multiple_of(v * 4, 4), 4)

    def block_of(place):
        other, steps = ORDER[place]
        return lax.rem(z + other, 2) * 4 + up_to(x + steps, 4)

    def gradients(place):
        block = block_of(place)

        @pl.loop(0, 32)
        def _(i):
            pair = block * 2 + i // 16
            core = lax.rem(i // 8, 2)
            rows = pl.ds(pl.multiple_of(lax.rem(i, 8) * 16, 16), 16)
            flat = pl.ds(pl.multiple_of(place * B + i * 16, 16), 16)
            gate = act[0, pair, core, rows].astype(F32)
            up = act[1, pair, core, rows].astype(F32)
            grad = gh[flat].astype(F32)
            sig = jax.nn.sigmoid(gate)
            value = gate * sig
            act[0, pair, core, rows] = (value * up).astype(BF16)
            act[1, pair, core, rows] = (grad * up * sig * (1.0 + gate * (1.0 - sig))).astype(BF16)
            gh[flat] = (grad * value).astype(BF16)

    def input_terms(place, store):
        block = block_of(place)

        @pl.loop(0, 2)
        def _(i):
            grad_gate = act[1, block * 2 + i].reshape(256, B)
            grad_up = gh[pl.ds(pl.multiple_of(place * B + i * 256, 256), 256)]
            store(
                pl.ds(pl.multiple_of(i * 256, 256), 256),
                lax.dot_general(grad_gate, wg_ref[...], NT, preferred_element_type=F32)
                + lax.dot_general(grad_up, wu_ref[...], NT, preferred_element_type=F32),
            )

    def kept(n):
        def store(rows, value):
            acc[n, rows] = value
        return store

    def sent(n):
        def store(rows, value):
            x_out[n, rows] = value.astype(BF16)
        return store

    def sent_with(n, m):
        def store(rows, value):
            x_out[n, rows] = (value + x_in[m, rows].astype(F32)).astype(BF16)
        return store

    def weight_grads(places, which, out_ref, last):
        scale = (8 * B) ** -0.5

        @pl.loop(0, 2)
        def _(i):
            rows = pl.ds(pl.multiple_of(i * 256, 256), 256)
            total = None
            for place in places:
                block = block_of(place)
                if which == 0:
                    left = act[0, pl.ds(block * 2, 2), :, :, rows].reshape(B, 256)
                    right = go[place]
                else:
                    left = inp[place, :, rows]
                    if which == 1:
                        right = act[1, pl.ds(block * 2, 2)].reshape(B, B)
                    else:
                        right = gh[pl.ds(place * B, B)]
                term = lax.dot_general(left, right, TN, preferred_element_type=F32)
                total = term if total is None else total + term
            if last:
                if len(places) < 8:
                    total = total + acc[2, rows]
                out_ref[rows] = (total * scale).astype(BF16)
            else:
                acc[2, rows] = total

    go_own = gather_own(go_ref, go)
    go[AT[0, 0]] = go_ref[...]
    inp[AT[0, 0]] = in_ref[...]
    mine = y * 4 + h
    act[0, mine, k] = gate_ref[...]
    act[1, mine, k] = up_ref[...]
    arrived(go_own[0], go_own[1])
    go_far = gather_far(go, 0)
    arrived(go_own[2])
    go_pair = gather_pair(go)
    ref = act.at[:, mine, k]
    act_h = send(ref, ref, h_right), send(ref, ref, h_left)

    core0 = products(0)
    arrived(*act_h)
    ref = act.at[0, y * 4 + h_prev, k]
    act_h2 = send(ref, ref, h_right)
    ref = act.at[1, y * 4 + h_next, k]
    act_h3 = send(ref, ref, h_left)
    arrived(core0)
    ya0 = y_first(0)
    yb0 = y_second(0, ya0)
    arrived(*go_far)
    go_last = send(go.at[AT[0, 2]], go.at[AT[1, 2]], z_pair)
    arrived(act_h2, act_h3)
    ref = act.at[:, act_rows(y), k]
    act_y = send(ref, ref, y_right), send(ref, ref, y_left)
    ha0 = h_first(0, (ya0[2], ya0[3]) + yb0)
    arrived(*go_pair)
    in_own = gather_own(in_ref, inp)
    arrived(go_last)
    core1 = products(1)
    hb0 = h_last(0, ha0)
    arrived(*act_y)
    ref = act.at[0, act_rows(y_prev), k]
    act_y2 = send(ref, ref, y_right)
    ref = act.at[1, act_rows(y_next), k]
    act_y3 = send(ref, ref, y_left)
    arrived(core1)
    ya1 = y_first(1)
    yc0 = y_gather(0, hb0)
    arrived(in_own[0], in_own[1])
    in_far = gather_far(inp, 0)
    arrived(in_own[2])
    in_pair = gather_pair(inp)
    yb1 = y_second(1, ya1)
    yd0 = y_forward(0, yc0)
    twins = []
    for v in (y, y_prev, y_next):
        ref = act.at[:, act_rows(v), k]
        twins.append(send(ref, ref, twin))
    ha1 = h_first(1, (ya1[2], ya1[3]) + yb1)
    ye0 = y_last(0, yd0)
    arrived(act_y2, act_y3)
    ref = act.at[:, act_rows(y_far), k]
    twins.append(send(ref, ref, twin))
    hb1 = h_last(1, ha1)
    arrived(yc0[2], yd0[1], yd0[3], ye0)
    arrived(*twins)
    yc1 = y_gather(1, hb1)
    arrived(*in_pair)
    in_far1 = gather_far(inp, 1)
    gone(*act_h, act_h2, act_h3, *act_y, act_y2, act_y3, *twins)
    gone(*hb0, *yc0, *yd0, ye0)
    for place in (2, 3):
        gradients(place)
        input_terms(place, sent(place - 2))
        if place == 2:
            x0 = send(x_out.at[0], x_in.at[0], x_right)
        else:
            x1 = send(x_out.at[1], x_in.at[1], x_left)
    yd1 = y_forward(1, yc1)
    for place in (0, 1):
        gradients(place)
        input_terms(place, kept(place))
    ye1 = y_last(1, yd1)
    weight_grads((0, 1, 2, 3), 0, dg_ref, False)
    arrived(yc1[2], yd1[1], yd1[3], ye1)
    gone(*hb1, *yc1, *yd1, ye1)
    gradients(7)
    input_terms(7, sent(2))
    x2 = send(x_out.at[2], x_in.at[2], z_pair)
    gradients(5)
    input_terms(5, sent(3))
    x3 = send(x_out.at[3], x_in.at[3], x_right)
    gradients(6)
    input_terms(6, sent(4))
    x4 = send(x_out.at[4], x_in.at[4], x_left)
    gradients(4)
    arrived(x2)
    input_terms(4, sent_with(5, 2))
    x5 = send(x_out.at[5], x_in.at[5], x_far)
    weight_grads((4, 5, 6, 7), 0, dg_ref, True)
    arrived(x3, x4)
    for i in range(2):
        rows = pl.ds(i * 256, 256)
        x_out[6, rows] = (acc[1, rows] + x_in[3, rows].astype(F32) + x_in[4, rows].astype(F32)).astype(BF16)
    x6 = send(x_out.at[6], x_in.at[6], z_pair)
    arrived(*in_far, *in_far1)
    weight_grads(tuple(range(8)), 1, gg_ref, True)
    weight_grads(tuple(range(8)), 2, ug_ref, True)
    arrived(x0, x1, x5, x6)
    for i in range(2):
        rows = pl.ds(i * 256, 256)
        total = acc[0, rows]
        for n in (0, 1, 5, 6):
            total = total + x_in[n, rows].astype(F32)
        ig_ref[rows] = total.astype(BF16)
    gone(*range(len(copies)))


def per_device(*args):
    vmem = pl.BlockSpec(memory_space=pltpu.VMEM)
    block = jax.ShapeDtypeStruct((B, B), BF16)
    return tuple(pl.pallas_call(
        kernel,
        name="slab_backward",
        out_shape=(block,) * 4,
        in_specs=[vmem] * 7,
        out_specs=(vmem,) * 4,
        scratch_shapes=[
            pltpu.VMEM((8, B, B), BF16),
            pltpu.VMEM((8, B, B), BF16),
            pltpu.VMEM((2, 16, 2, ROWS, B), BF16),
            pltpu.VMEM((8 * B, B), BF16),
            pltpu.VMEM((2, 2 * B, B), F32),
            pltpu.VMEM((2, 2 * B, B), F32),
            pltpu.VMEM((2, 2 * B, B), F32),
            pltpu.VMEM((2, 3, 256, B), BF16),
            pltpu.VMEM((2, 2, 128, B), BF16),
            pltpu.VMEM((2, 2, 256, B), BF16),
            pltpu.VMEM((2, 256, B), F32),
            pltpu.VMEM((2, 3, 64, B), F32),
            pltpu.VMEM((7, B, B), BF16),
            pltpu.VMEM((7, B, B), BF16),
            pltpu.VMEM((3, B, B), F32),
            pltpu.SemaphoreType.DMA((96,)),
            pltpu.SemaphoreType.DMA((96,)),
        ],
        compiler_params=pltpu.CompilerParams(
            collective_id=0, has_side_effects=True, vmem_limit_bytes=60 * 1024 * 1024
        ),
        cost_estimate=pl.CostEstimate(flops=12 * 4096 * B * B, bytes_accessed=12 * B * B, transcendentals=4096 * B),
    )(*args))


def solution(mesh):
    placed = (
        P("col", "row"),
        P("col", "row"),
        P("row", "col"),
        P("row", "col"),
        P("row", "col"),
        P("row", "col"),
        P("col", "row"),
    )
    return jax.shard_map(
        per_device,
        mesh=mesh,
        in_specs=placed,
        out_specs=(P("col", "row"), P("row", "col"), P("row", "col"), P("col", "row")),
        check_vma=False,
    )
```

time: 541 us -> 182 us (0.34)
  the two profiles are of different devices: /device:TPU:1 before, /device:TPU:2 now
where the time goes in v1:
time: 182 us
  Pallas kernels  176 us (97%)
  local copies, waits for them, and re-layouts  5.18 us (3%)
    pallas_call x1, Pallas kernels, per_device(): pl.pallas_call(kernel, name='slab_backward', out_shape=(block,) * 4, in_s...  176 us
    unnamed x10, local copies, waits for them, and re-layouts  5.18 us

profile of v1, /device:TPU:2, one launch (start us, length us, event | category | flops | bytes accessed | tf_op | source)
XLA Modules:
  0.0 182.2 jit_solution(7524610125162502767)
XLA Ops:
  0.6 176.3 %slab_backward.1 = (bf16[512,512]{1,0:T(8,128)(2,1)}, bf16[512,512]{1,0:T(8,128)(2,1)}, bf16[512,512]{1,0:T(8,128)(2,1)}, bf16[512,512]{1,0:T(8,128)(2,1)}) custom-call(bf16[512,512]{1,0:T(8,128)(2,1)} %go_ref.1, bf16[512,512]{1,0:T(8,128)(2,1)} %in_ref.1, bf16[128,512]{1,0:T(8,128)(2,1)} %gate_ref.1, bf16[128,512]{1,0:T(8,128)(2,1)} %up_ref.1, ...), custom_call_target="tpu_custom_call" | custom-call | flops 12884901888 | bytes 3145728 | tf_op jit(solution)/shard_map/slab_backward/pallas_call | solution.py:375
  177.0 0.0 copy-start.2
  177.0 1.9 %copy.15 = bf16[512,512]{1,0:T(8,128)(2,1)} copy(bf16[512,512]{1,0:T(8,128)(2,1)} %get-tuple-element.8) | data formatting | bytes 1048576
  178.9 0.0 copy-done.2
  178.9 0.0 copy-start.1
  178.9 0.8 copy.16
  179.7 0.4 copy-done.1
  180.1 0.0 copy-start
  180.1 0.8 copy.17
  180.9 0.4 copy-done
  181.4 0.8 copy.18
Async XLA Ops:
  177.0 1.9 %copy-start.2 = (bf16[512,512]{1,0:T(8,128)(2,1)S(1)}, bf16[512,512]{1,0:T(8,128)(2,1)}, u32[]{:S(2)}) copy-start(bf16[512,512]{1,0:T(8,128)(2,1)} %get-tuple-element.9) | copy-start | bytes 1572868
  178.9 1.2 copy-start.1
  180.1 1.2 copy-start

commit v2 on v0

v2 whole, which is shorter than its diff:
```python
import functools

import jax
import jax.numpy as jnp
from jax import lax
from jax.experimental import pallas as pl
from jax.experimental.pallas import tpu as pltpu
from jax.sharding import PartitionSpec as P

MESH = pl.DeviceIdType.MESH
F32, BF16 = jnp.float32, jnp.bfloat16
B = 512
ROWS = 128
ORDER = ((0, 1), (0, 3), (1, 1), (1, 3), (0, 2), (1, 2), (0, 0), (1, 0))
AT = {where: place for place, where in enumerate(ORDER)}
GROUPS = 4
HALF = 8 * B // GROUPS // 2
YR = HALF // 4
HR = YR // 4
FAR = "go4"
INS = ("in0", "in3", "in1", "in2", "in4")
ACTS = ("a0", "a1", "a2", "a3", "bp", "bn", "bf", "cp", "cn", "cf", "t0", "t1", "t2")
SCHEDULE = (
    "go1", "go0", "go3", "a0", "a1", "P0", "Y0", "P3", "Y3", "a3",
    "in1", "go2", "Z0", "a2", "go4", "bp", "P1", "bn", "Y1", "t0",
    "in0", "Z1", "P2", "H0", "bf", "Y2", "H1", "in3", "Z2", "cn",
    "I1", "cp", "H2", "J1", "in4", "cf", "in2", "t1", "I0", "K1",
    "I2", "Z3", "t2", "J0", "L1", "H3", "J2", "R1", "u11a", "u13b",
    "u11b", "K0", "u13a", "K2", "I3", "L0", "L2", "R0", "u01a", "R2",
    "u12a", "u03b", "u12b", "J3", "u01b", "u03a", "w0", "K3", "d0", "v02b",
    "L3", "R3", "u10a", "s1a", "u02b", "v02a", "u10b", "s1b", "u02a", "u00b",
    "g0", "u00a", "w1", "d1", "g1", "s0b", "s0a",
)
NT = (((1,), (1,)), ((), ()))
TN = (((0,), (0,)), ((), ()))


def kernel(
    go_hbm, in_hbm, gate_hbm, up_hbm, wg_hbm, wu_hbm, wd_hbm,
    ig_hbm, gg_hbm, ug_hbm, dg_hbm,
    weights_in, results, go, inp, act, gh, part, own, core_in,
    y_out, y_mid, y_in, h_sum, h_in, x_out, x_in, acc, held,
    send_sem, recv_sem, local_sem,
):
    row, col = lax.axis_index("row"), lax.axis_index("col")
    k, h, y = lax.rem(row, 2), lax.rem(row // 2, 4), row // 8
    x, z = lax.rem(col, 4), col // 4

    def row_of(y_, h_, k_):
        return (y_ * 4 + h_) * 2 + k_

    x_right, x_left, x_far = ((row, z * 4 + lax.rem(x + d, 4)) for d in (1, 3, 2))
    z_pair = (row, (1 - z) * 4 + x)
    y_next, y_prev, y_far = (lax.rem(y + d, 4) for d in (1, 3, 2))
    y_right, y_left = ((row_of(v, h, k), col) for v in (y_next, y_prev))
    h_next, h_prev, h_far = (lax.rem(h + d, 4) for d in (1, 3, 2))
    h_right, h_left, h_over = ((row_of(y, v, k), col) for v in (h_next, h_prev, h_far))
    twin = (row_of(y, h, 1 - k), col)
    friends = (x_right, x_left, x_far, z_pair, y_right, y_left, h_right, h_left, h_over, twin)

    mine = y * 4 + h
    loads = [
        pltpu.make_async_copy(src, dst, local_sem.at[n])
        for n, (src, dst) in enumerate((
            (go_hbm, go.at[AT[0, 0]]),
            (gate_hbm, act.at[0, mine, k]),
            (up_hbm, act.at[1, mine, k]),
            (wd_hbm, weights_in.at[2]),
            (in_hbm, inp.at[AT[0, 0]]),
            (wg_hbm, weights_in.at[0]),
            (wu_hbm, weights_in.at[1]),
        ))
    ]
    for load in loads:
        load.start()
    wg_ref, wu_ref, wd_ref = (weights_in.at[n] for n in range(3))
    ig_ref, gg_ref, ug_ref, dg_ref = (results.at[n] for n in range(4))

    barrier = pltpu.get_barrier_semaphore()
    for friend in friends:
        pl.semaphore_signal(barrier, inc=1, device_id=friend, device_id_type=MESH)
    pl.semaphore_wait(barrier, len(friends))

    for load in loads[:3]:
        load.wait()
    copies = []
    made = {}
    tasks = {}

    def send(src, dst, to):
        n = len(copies)
        copy = pltpu.make_async_remote_copy(
            src_ref=src, dst_ref=dst, send_sem=send_sem.at[n], recv_sem=recv_sem.at[n],
            device_id=to, device_id_type=MESH,
        )
        copy.start()
        copies.append([copy, False, False])
        return n

    waited = [True] * 3 + [False] * 4

    def loaded(n):
        if not waited[n]:
            loads[n].wait()
            waited[n] = True

    def arrived(*ns):
        for n in ns:
            if not copies[n][2]:
                copies[n][0].wait_recv()
                copies[n][2] = True

    def gone(*ns):
        for n in ns:
            if not copies[n][1]:
                copies[n][0].wait_send()
                copies[n][1] = True

    def task(name):
        def add(run):
            def step():
                made[name] = run()
            tasks[name] = step
            return run
        return add

    def at(start, n, step):
        return pl.ds(pl.multiple_of(start, step), n)

    first, second = pl.ds(0, B // 2), pl.ds(B // 2, B // 2)

    saves = []

    def save(n, rows=slice(None)):
        copy = pltpu.make_async_copy(
            results.at[n, rows], (ig_hbm, gg_hbm, ug_hbm, dg_hbm)[n].at[rows], local_sem.at[len(loads) + len(saves)]
        )
        copy.start()
        saves.append(copy)

    def gather(name, load, buf):
        src = buf.at[AT[0, 0]]

        @task(name + "0")
        def _():
            loaded(load)
            return (
                send(src, buf.at[AT[0, 3]], x_right),
                send(src, buf.at[AT[0, 1]], x_left),
            )

        @task(name + "1")
        def _():
            loaded(load)
            return (send(src, buf.at[AT[1, 0]], z_pair),)

        def far(plane):
            return (
                send(buf.at[AT[plane, 3], first], buf.at[AT[plane, 2], first], x_right),
                send(buf.at[AT[plane, 1], second], buf.at[AT[plane, 2], second], x_left),
            )

        @task(name + "2")
        def _():
            arrived(*made[name + "0"])
            return far(0)

        @task(name + "3")
        def _():
            arrived(*made[name + "1"])
            return (
                send(buf.at[AT[1, 0]], buf.at[AT[1, 3]], x_right),
                send(buf.at[AT[1, 0]], buf.at[AT[1, 1]], x_left),
            )

        @task(name + "4")
        def _():
            arrived(*made[name + "3"])
            return far(1)

        @task(name + "z")
        def _():
            arrived(*made[name + "2"])
            return (send(buf.at[AT[0, 2]], buf.at[AT[1, 2]], z_pair),)

    gather("go", 0, go)
    gather("in", 4, inp)

    @task("a0")
    def _():
        ref = act.at[:, mine, k]
        return send(ref, ref, h_right), send(ref, ref, h_left)

    def act_to_y(h_):
        ref = act.at[:, y * 4 + h_, k]
        return send(ref, ref, y_right), send(ref, ref, y_left)

    def act_on_y(h_):
        ref = act.at[0, y_prev * 4 + h_, k]
        n = send(ref, ref, y_right)
        ref = act.at[1, y_next * 4 + h_, k]
        return n, send(ref, ref, y_left)

    @task("a1")
    def _():
        return act_to_y(h)

    @task("a2")
    def _():
        arrived(*made["a0"])
        ref = act.at[0, y * 4 + h_prev, k]
        n = send(ref, ref, h_right)
        ref = act.at[1, y * 4 + h_next, k]
        return n, send(ref, ref, h_left)

    @task("a3")
    def _():
        arrived(*made["a1"])
        return act_on_y(h)

    for name, h_, source in (("p", h_prev, "a0"), ("n", h_next, "a0"), ("f", h_far, "a2")):
        def pair(name=name, h_=h_, source=source):
            @task("b" + name)
            def _():
                arrived(*made[source])
                return act_to_y(h_)

            @task("c" + name)
            def _():
                arrived(*made["b" + name])
                return act_on_y(h_)
        pair()

    def act_twin(y_):
        ref = act.at[:, at(y_ * 4, 4, 4), k]
        return send(ref, ref, twin)

    @task("t0")
    def _():
        arrived(*made["a0"], *made["a2"])
        return (act_twin(y),)

    @task("t1")
    def _():
        arrived(*made["a1"], *made["bp"], *made["bn"], *made["bf"])
        return act_twin(y_prev), act_twin(y_next)

    @task("t2")
    def _():
        arrived(*made["a3"], *made["cp"], *made["cn"], *made["cf"])
        return (act_twin(y_far),)

    needs = (("go0",), ("go3",), ("go2", FAR), ("go1",))

    def product(g, half, to):
        step = min(256, HALF)

        @pl.loop(0, HALF // step)
        def _(i):
            place = g * 2 + half
            tile = go[place, at(i * step, step, step)]
            to[g, at(i * step, step, step)] = lax.dot_general(
                tile, wd_ref[...], NT, preferred_element_type=F32
            )

    def pair_sum(g, v, lo, n):
        rows = at(v * YR + lo, n, 64)
        return own[g, rows] + core_in[g, rows]

    lo, hi = pl.ds(0, YR // 2), pl.ds(YR // 2, YR // 2)

    def gh_rows(g, y_, start, n):
        return gh.at[at(g * 2 * HALF + k * HALF + y_ * YR + start, n, HR)]

    def summed(g):
        t = str(g)

        @task("P" + t)
        def _():
            for name in needs[g]:
                arrived(*made[name])
            loaded(3)
            product(g, 1 - k, part)
            n = send(part.at[g], core_in.at[g], twin)
            product(g, k, own)
            return (n,)

        @task("Y" + t)
        def _():
            arrived(*made["P" + t])
            y_out[g, 0] = pair_sum(g, y_far, 0, YR).astype(BF16)
            a = send(y_out.at[g, 0, lo], y_mid.at[g, 0], y_right)
            b = send(y_out.at[g, 0, hi], y_mid.at[g, 1], y_left)
            y_out[g, 1, hi] = pair_sum(g, y_next, YR // 2, YR // 2).astype(BF16)
            c = send(y_out.at[g, 1, hi], y_in.at[g, 0, hi], y_right)
            y_out[g, 2, lo] = pair_sum(g, y_prev, 0, YR // 2).astype(BF16)
            d = send(y_out.at[g, 2, lo], y_in.at[g, 1, lo], y_left)
            return a, b, c, d

        @task("Z" + t)
        def _():
            a, b, c, d = made["Y" + t]
            arrived(a)
            y_out[g, 1, lo] = (pair_sum(g, y_next, 0, YR // 2) + y_mid[g, 0].astype(F32)).astype(BF16)
            e = send(y_out.at[g, 1, lo], y_in.at[g, 0, lo], y_right)
            arrived(b)
            y_out[g, 2, hi] = (pair_sum(g, y_prev, YR // 2, YR // 2) + y_mid[g, 1].astype(F32)).astype(BF16)
            f = send(y_out.at[g, 2, hi], y_in.at[g, 1, hi], y_left)
            h_sum[g] = pair_sum(g, y, 0, YR)
            return c, d, e, f

        @task("H" + t)
        def _():
            arrived(*made["Z" + t])
            h_sum[g] = h_sum[g] + y_in[g, 0].astype(F32) + y_in[g, 1].astype(F32)

            def piece(v):
                return h_sum.at[g, at(v * HR, HR, HR)]

            return (
                send(piece(h_far), h_in.at[g, 2], h_over),
                send(piece(h_next), h_in.at[g, 0], h_right),
                send(piece(h_prev), h_in.at[g, 1], h_left),
            )

        @task("I" + t)
        def _():
            arrived(*made["H" + t])
            total = h_sum[g, at(h * HR, HR, HR)] + h_in[g, 0] + h_in[g, 1] + h_in[g, 2]
            ref = gh_rows(g, y, h * HR, HR)
            ref[...] = total.astype(BF16)
            return tuple(send(ref, ref, to) for to in (h_over, h_right, h_left))

        @task("J" + t)
        def _():
            arrived(*made["I" + t])
            ref = gh_rows(g, y, 0, YR)
            return tuple(send(ref, ref, to) for to in (y_right, y_left, twin))

        @task("K" + t)
        def _():
            a, b, c = made["J" + t]
            arrived(a)
            ref = gh_rows(g, y_prev, 0, YR // 2)
            d = send(ref, ref, y_right)
            ref = gh_rows(g, y_prev, 0, YR)
            e = send(ref, ref, twin)
            arrived(b)
            ref = gh_rows(g, y_next, YR // 2, YR // 2)
            f = send(ref, ref, y_left)
            ref = gh_rows(g, y_next, 0, YR)
            i = send(ref, ref, twin)
            return d, f, c, e, i

        @task("L" + t)
        def _():
            d, f, c, e, i = made["K" + t]
            arrived(d, f)
            ref = gh_rows(g, y_far, 0, YR)
            return c, e, i, send(ref, ref, twin)

        @task("R" + t)
        def _():
            arrived(*made["L" + t])
            for name in ("I", "J", "K", "L"):
                gone(*made[name + t])
            for name in ACTS:
                arrived(*made[name])
                gone(*made[name])

    for g in range(GROUPS):
        summed(g)

    def block_of(place):
        other, steps = ORDER[place]
        return lax.rem(z + other, 2) * 4 + lax.rem(x + steps, 4)

    def gradients(place, half):
        block = block_of(place)

        @pl.loop(half * 16, half * 16 + 16, unroll=2)
        def _(i):
            pair = block * 2 + i // 16
            core = lax.rem(i // 8, 2)
            rows = at(lax.rem(i, 8) * 16, 16, 16)
            flat = at(place * B + i * 16, 16, 16)
            gate = act[0, pair, core, rows].astype(F32)
            up = act[1, pair, core, rows].astype(F32)
            grad = gh[flat].astype(F32)
            sig = 0.5 * jnp.tanh(0.5 * gate) + 0.5
            value = gate * sig
            act[0, pair, core, rows] = (value * up).astype(BF16)
            act[1, pair, core, rows] = (grad * up * sig * (1.0 + gate * (1.0 - sig))).astype(BF16)
            gh[flat] = (grad * value).astype(BF16)

    def input_terms(place, half):
        loaded(5)
        loaded(6)
        grad_gate = act[1, block_of(place) * 2 + half].reshape(256, B)
        grad_up = gh[pl.ds(place * B + half * 256, 256)]
        gate_term = lax.dot_general(grad_gate, wg_ref[...], NT, preferred_element_type=F32)
        return gate_term + lax.dot_general(grad_up, wu_ref[...], NT, preferred_element_type=F32)

    halves = ((0, "a", first), (1, "b", second))

    def out(name, n, where, to):
        for half, t, rows in halves:
            def one(half=half, t=t, rows=rows):
                @task("u" + name + t)
                def _():
                    gradients(AT[where], half)
                    x_out[n, rows] = input_terms(AT[where], half).astype(BF16)
                    return (send(x_out.at[n, rows], x_in.at[n, rows], to),)
            one()

    out("01", 0, (0, 1), x_right)
    out("03", 1, (0, 3), x_left)
    out("11", 3, (1, 1), x_right)
    out("13", 4, (1, 3), x_left)
    out("12", 2, (1, 2), z_pair)

    def rest(half, t, rows):
        @task("v02" + t)
        def _():
            gradients(AT[0, 2], half)

        @task("u02" + t)
        def _():
            arrived(*made["u12" + t])
            total = input_terms(AT[0, 2], half) + x_in[2, rows].astype(F32)
            x_out[5, rows] = total.astype(BF16)
            return (send(x_out.at[5, rows], x_in.at[5, rows], x_far),)

        @task("u00" + t)
        def _():
            gradients(AT[0, 0], half)
            acc[0, rows] = input_terms(AT[0, 0], half)

        @task("u10" + t)
        def _():
            gradients(AT[1, 0], half)
            acc[1, rows] = input_terms(AT[1, 0], half)

        @task("s1" + t)
        def _():
            arrived(*made["u11" + t], *made["u13" + t])
            total = acc[1, rows] + x_in[3, rows].astype(F32) + x_in[4, rows].astype(F32)
            x_out[6, rows] = total.astype(BF16)
            return (send(x_out.at[6, rows], x_in.at[6, rows], z_pair),)

        @task("s0" + t)
        def _():
            arrived(*made["u01" + t], *made["u03" + t], *made["u02" + t], *made["s1" + t])
            total = acc[0, rows]
            for n in (0, 1, 5, 6):
                total = total + x_in[n, rows].astype(F32)
            ig_ref[rows] = total.astype(BF16)
            return save(0, rows)

    for half, t, rows in halves:
        rest(half, t, rows)

    def weight_grads(places, which, out_ref, last):
        scale = (8 * B) ** -0.5

        @pl.loop(0, 2)
        def _(i):
            rows = at(i * 256, 256, 256)
            total = None
            for place in places:
                block = block_of(place)
                if which == 0:
                    left = act[0, pl.ds(block * 2, 2), :, :, rows].reshape(B, 256)
                    right = go[place]
                else:
                    left = inp[place, :, rows]
                    if which == 1:
                        right = act[1, pl.ds(block * 2, 2)].reshape(B, B)
                    else:
                        right = gh[pl.ds(place * B, B)]
                term = lax.dot_general(left, right, TN, preferred_element_type=F32)
                total = term if total is None else total + term
            if last:
                out_ref[rows] = ((total + held[which, rows]) * scale).astype(BF16)
            else:
                held[which, rows] = total

    def weights(name, which, out_ref):
        @task(name + "0")
        def _():
            if which:
                for n in INS[:2]:
                    arrived(*made[n])
            weight_grads((0, 1, 2, 3), which, out_ref, False)

        @task(name + "1")
        def _():
            if which:
                for n in INS:
                    arrived(*made[n])
            weight_grads((4, 5, 6, 7), which, out_ref, True)
            save((3, 1, 2)[which])

    weights("d", 0, dg_ref)
    weights("g", 1, gg_ref)
    weights("w", 2, ug_ref)

    for name in SCHEDULE:
        tasks[name]()
    arrived(*range(len(copies)))
    gone(*range(len(copies)))
    for copy in saves:
        copy.wait()


def handed_on(*refs):
    held, sems = refs[8:]
    ins = [pltpu.make_async_copy(refs[n], held.at[n], sems.at[n]) for n in range(4)]
    outs = [pltpu.make_async_copy(held.at[n], refs[4 + n], sems.at[4 + n]) for n in range(4)]
    for move in ins:
        move.start()
    for n in range(4):
        ins[n].wait()
        outs[n].start()
    for move in outs:
        move.wait()


def per_device(*args):
    hbm = pl.BlockSpec(memory_space=pl.ANY)
    block = jax.ShapeDtypeStruct((B, B), BF16)
    made = pl.pallas_call(
        kernel,
        name="slab_backward",
        out_shape=(block,) * 4,
        in_specs=[hbm] * 7,
        out_specs=(hbm,) * 4,
        scratch_shapes=[
            pltpu.VMEM((3, B, B), BF16),
            pltpu.VMEM((4, B, B), BF16),
            pltpu.VMEM((8, B, B), BF16),
            pltpu.VMEM((8, B, B), BF16),
            pltpu.VMEM((2, 16, 2, ROWS, B), BF16),
            pltpu.VMEM((8 * B, B), BF16),
            pltpu.VMEM((GROUPS, HALF, B), F32),
            pltpu.VMEM((GROUPS, HALF, B), F32),
            pltpu.VMEM((GROUPS, HALF, B), F32),
            pltpu.VMEM((GROUPS, 3, YR, B), BF16),
            pltpu.VMEM((GROUPS, 2, YR // 2, B), BF16),
            pltpu.VMEM((GROUPS, 2, YR, B), BF16),
            pltpu.VMEM((GROUPS, YR, B), F32),
            pltpu.VMEM((GROUPS, 3, HR, B), F32),
            pltpu.VMEM((7, B, B), BF16),
            pltpu.VMEM((7, B, B), BF16),
            pltpu.VMEM((2, B, B), F32),
            pltpu.VMEM((3, B, B), F32),
            pltpu.SemaphoreType.DMA((160,)),
            pltpu.SemaphoreType.DMA((160,)),
            pltpu.SemaphoreType.DMA((12,)),
        ],
        compiler_params=pltpu.CompilerParams(
            collective_id=0, has_side_effects=True, vmem_limit_bytes=60 * 1024 * 1024
        ),
        cost_estimate=pl.CostEstimate(flops=12 * 4096 * B * B, bytes_accessed=12 * B * B, transcendentals=4096 * B),
    )(*args)
    return tuple(pl.pallas_call(
        handed_on,
        name="hand_on",
        out_shape=(block,) * 4,
        in_specs=[hbm] * 4,
        out_specs=(hbm,) * 4,
        scratch_shapes=[pltpu.VMEM((4, B, B), BF16), pltpu.SemaphoreType.DMA((8,))],
        compiler_params=pltpu.CompilerParams(vmem_limit_bytes=60 * 1024 * 1024),
    )(*made))


def solution(mesh):
    placed = (
        P("col", "row"),
        P("col", "row"),
        P("row", "col"),
        P("row", "col"),
        P("row", "col"),
        P("row", "col"),
        P("col", "row"),
    )
    return jax.shard_map(
        per_device,
        mesh=mesh,
        in_specs=placed,
        out_specs=(P("col", "row"), P("row", "col"), P("row", "col"), P("col", "row")),
        check_vma=False,
    )
```

time: 541 us -> 130 us (0.24)
  waiting for transfers between devices: 476 us -> 0 us
  Pallas kernels: 0 us -> 129 us
  matrix products: 44.1 us -> 0 us
  between operations: 14.2 us -> 0.64 us
    all_gather x5 -> x0, waiting for transfers between devices: 266 us -> none  [the longest x1 60.9 us: per_device(): lax.all_gather(grad_out, 'col', axis=0, tiled=True)]
    reduce_scatter x2 -> x0, waiting for transfers between devices: 208 us -> none  [the longest x1 120 us: per_device(): lax.psum_scatter(times_transposed(grad_rows, w_down), 'row', scatter_dime...]
    pallas_call x0 -> x2, Pallas kernels: none -> 129 us  [the longest x1 127 us: per_device(): pl.pallas_call(kernel, name='slab_backward', out_shape=(block,) * 4, in_s...]
    dot_general x6 -> x0, matrix products: 44.1 us -> none  [the longest x3 25.9 us: times_transposed(): lax.dot_general(left, right, (((1,), (1,)), ((), ())), preferred_element_...]
  transfers between devices with their start and end apart: 7 -> 0, of which waited for: 7 -> 0; matrix products, arithmetic and copies ran while one was open for 7% -> 0% of each run, Pallas kernels for 0% -> 0%
where the time goes in v2:
time: 130 us
  Pallas kernels  129 us (99%)
    pallas_call x1, Pallas kernels, per_device(): pl.pallas_call(kernel, name='slab_backward', out_shape=(block,) * 4, in_s...  127 us

profile of v2, /device:TPU:1, one launch (start us, length us, event | category | flops | bytes accessed | tf_op | source)
XLA Modules:
  0.0 130.1 jit_solution(180586901334818557)
XLA Ops:
  0.6 127.0 %slab_backward.1 = (bf16[512,512]{1,0:T(8,128)(2,1)}, bf16[512,512]{1,0:T(8,128)(2,1)}, bf16[512,512]{1,0:T(8,128)(2,1)}, bf16[512,512]{1,0:T(8,128)(2,1)}) custom-call(bf16[512,512]{1,0:T(8,128)(2,1)} %go_hbm.1, bf16[512,512]{1,0:T(8,128)(2,1)} %in_hbm.1, bf16[128,512]{1,0:T(8,128)(2,1)} %gate_hbm.1, bf16[128,512]{1,0:T(8,128)(2,1)} %up_hbm.1, ...), custom_call_target="tpu_custom_call" | custom-call | flops 12884901888 | bytes 3145728 | tf_op jit(solution)/shard_map/slab_backward/pallas_call | solution.py:532
  127.7 2.4 %hand_on.1 = (bf16[512,512]{1,0:T(8,128)(2,1)}, bf16[512,512]{1,0:T(8,128)(2,1)}, bf16[512,512]{1,0:T(8,128)(2,1)}, bf16[512,512]{1,0:T(8,128)(2,1)}) custom-call(bf16[512,512]{1,0:T(8,128)(2,1)} %get-tuple-element.8.refs_0_, bf16[512,512]{1,0:T(8,128)(2,1)} %get-tuple-element.9.refs_1_, bf16[512,512]{1,0:T(8,128)(2,1)} %get-tuple-element.10.refs_2_, ...), custom_call_target="tpu_custom_call" | custom-call | tf_op jit(solution)/shard_map/hand_on/pallas_call | solution.py:566

commit v3 on v2

--- a/solution.py
+++ b/solution.py
@@ -17,19 +17,23 @@
 HALF = 8 * B // GROUPS // 2
 YR = HALF // 4
 HR = YR // 4
-FAR = "go4"
-INS = ("in0", "in3", "in1", "in2", "in4")
+X_RING, FAR_BY_X = False, False
+Y_DIRECT = False
+Y_TYPE, H_TYPE = BF16, BF16
+RING_IN, RING_OUT = False, False
+INS = ("in0a", "in0b", "in3a", "in3b", "in1a", "in1b", "in2a", "in2b", "in4a", "in4b")
 ACTS = ("a0", "a1", "a2", "a3", "bp", "bn", "bf", "cp", "cn", "cf", "t0", "t1", "t2")
 SCHEDULE = (
-    "go1", "go0", "go3", "a0", "a1", "P0", "Y0", "P3", "Y3", "a3",
-    "in1", "go2", "Z0", "a2", "go4", "bp", "P1", "bn", "Y1", "t0",
-    "in0", "Z1", "P2", "H0", "bf", "Y2", "H1", "in3", "Z2", "cn",
-    "I1", "cp", "H2", "J1", "in4", "cf", "in2", "t1", "I0", "K1",
-    "I2", "Z3", "t2", "J0", "L1", "H3", "J2", "R1", "u11a", "u13b",
-    "u11b", "K0", "u13a", "K2", "I3", "L0", "L2", "R0", "u01a", "R2",
-    "u12a", "u03b", "u12b", "J3", "u01b", "u03a", "w0", "K3", "d0", "v02b",
-    "L3", "R3", "u10a", "s1a", "u02b", "v02a", "u10b", "s1b", "u02a", "u00b",
-    "g0", "u00a", "w1", "d1", "g1", "s0b", "s0a",
+    "go1b", "a1", "go0a", "go0b", "go1a", "a3", "go3b", "a0", "P3", "go3a",
+    "P0", "Y3", "Y0", "Z3", "in1b", "in1a", "go4b", "go2a", "Z0", "P1",
+    "go2b", "bp", "a2", "go4a", "Y1", "Z1", "in0b", "bn", "in0a", "P2",
+    "H1", "cp", "in3a", "Y2", "I1", "bf", "Z2", "H0", "in3b", "in2a",
+    "H3", "F1", "t0", "cn", "H2", "J1", "in4a", "in2b", "I0", "cf",
+    "t1", "I2", "F0", "K1", "J0", "F2", "t2", "I3", "L1", "in4b",
+    "J2", "R1", "u13", "K0", "u11", "F3", "K2", "L0", "R0", "u01",
+    "L2", "J3", "R2", "v12", "u12b", "u03", "K3", "d0", "u12a", "w0",
+    "L3", "R3", "u10", "s1b", "s1a", "v02", "u02b", "u00", "g0", "u02a",
+    "g1", "w1", "d1", "s0b", "s0a",
 )
 NT = (((1,), (1,)), ((), ()))
 TN = (((0,), (0,)), ((), ()))
@@ -39,7 +43,7 @@
     go_hbm, in_hbm, gate_hbm, up_hbm, wg_hbm, wu_hbm, wd_hbm,
     ig_hbm, gg_hbm, ug_hbm, dg_hbm,
     weights_in, results, go, inp, act, gh, part, own, core_in,
-    y_out, y_mid, y_in, h_sum, h_in, x_out, x_in, acc, held,
+    y_out, y_in, h_sum, h_out, h_in, x_out, x_in, acc, held,
     send_sem, recv_sem, local_sem,
 ):
     row, col = lax.axis_index("row"), lax.axis_index("col")
@@ -52,11 +56,11 @@
     x_right, x_left, x_far = ((row, z * 4 + lax.rem(x + d, 4)) for d in (1, 3, 2))
     z_pair = (row, (1 - z) * 4 + x)
     y_next, y_prev, y_far = (lax.rem(y + d, 4) for d in (1, 3, 2))
-    y_right, y_left = ((row_of(v, h, k), col) for v in (y_next, y_prev))
+    y_right, y_left, y_over = ((row_of(v, h, k), col) for v in (y_next, y_prev, y_far))
     h_next, h_prev, h_far = (lax.rem(h + d, 4) for d in (1, 3, 2))
     h_right, h_left, h_over = ((row_of(y, v, k), col) for v in (h_next, h_prev, h_far))
     twin = (row_of(y, h, 1 - k), col)
-    friends = (x_right, x_left, x_far, z_pair, y_right, y_left, h_right, h_left, h_over, twin)
+    friends = (x_right, x_left, z_pair, y_right, y_left, h_right, h_left, h_over, twin) + ((y_over,) if Y_DIRECT else ()) + (() if X_RING else (x_far,))
 
     mine = y * 4 + h
     loads = [
@@ -138,50 +142,51 @@
         copy.start()
         saves.append(copy)
 
+    halves = ((0, "a", first), (1, "b", second))
+
     def gather(name, load, buf):
-        src = buf.at[AT[0, 0]]
-
-        @task(name + "0")
-        def _():
-            loaded(load)
-            return (
-                send(src, buf.at[AT[0, 3]], x_right),
-                send(src, buf.at[AT[0, 1]], x_left),
-            )
-
-        @task(name + "1")
-        def _():
-            loaded(load)
-            return (send(src, buf.at[AT[1, 0]], z_pair),)
-
-        def far(plane):
-            return (
-                send(buf.at[AT[plane, 3], first], buf.at[AT[plane, 2], first], x_right),
-                send(buf.at[AT[plane, 1], second], buf.at[AT[plane, 2], second], x_left),
-            )
-
-        @task(name + "2")
-        def _():
-            arrived(*made[name + "0"])
-            return far(0)
-
-        @task(name + "3")
-        def _():
-            arrived(*made[name + "1"])
-            return (
-                send(buf.at[AT[1, 0]], buf.at[AT[1, 3]], x_right),
-                send(buf.at[AT[1, 0]], buf.at[AT[1, 1]], x_left),
-            )
-
-        @task(name + "4")
-        def _():
-            arrived(*made[name + "3"])
-            return far(1)
-
-        @task(name + "z")
-        def _():
-            arrived(*made[name + "2"])
-            return (send(buf.at[AT[0, 2]], buf.at[AT[1, 2]], z_pair),)
+        mine = buf.at[AT[0, 0]]
+        paired = buf.at[AT[1, 0]]
+
+        def one(half, t, rows):
+            def both_ways(src, plane):
+                return (
+                    send(src, buf.at[AT[plane, 3], rows], x_right),
+                    send(src, buf.at[AT[plane, 1], rows], x_left),
+                )
+
+            def far(plane):
+                if half == 0:
+                    return (send(buf.at[AT[plane, 3], rows], buf.at[AT[plane, 2], rows], x_right),)
+                return (send(buf.at[AT[plane, 1], rows], buf.at[AT[plane, 2], rows], x_left),)
+
+            @task(name + "0" + t)
+            def _():
+                loaded(load)
+                return both_ways(mine.at[rows], 0)
+
+            @task(name + "1" + t)
+            def _():
+                loaded(load)
+                return (send(mine.at[rows], buf.at[AT[1, 0], rows], z_pair),)
+
+            @task(name + "2" + t)
+            def _():
+                arrived(made[name + "0" + t][half])
+                return far(0)
+
+            @task(name + "3" + t)
+            def _():
+                arrived(*made[name + "1" + t])
+                return both_ways(paired.at[rows], 1)
+
+            @task(name + "4" + t)
+            def _():
+                arrived(made[name + "3" + t][half])
+                return far(1)
+
+        for half, t, rows in halves:
+            one(half, t, rows)
 
     gather("go", 0, go)
     gather("in", 4, inp)
@@ -250,18 +255,10 @@
         arrived(*made["a3"], *made["cp"], *made["cn"], *made["cf"])
         return (act_twin(y_far),)
 
-    needs = (("go0",), ("go3",), ("go2", FAR), ("go1",))
+    needs = (("go0a", "go0b"), ("go3a", "go3b"), ("go2a", "go2b", "go4a", "go4b"), ("go1a", "go1b"))
 
     def product(g, half, to):
-        step = min(256, HALF)
-
-        @pl.loop(0, HALF // step)
-        def _(i):
-            place = g * 2 + half
-            tile = go[place, at(i * step, step, step)]
-            to[g, at(i * step, step, step)] = lax.dot_general(
-                tile, wd_ref[...], NT, preferred_element_type=F32
-            )
+        to[g] = lax.dot_general(go[g * 2 + half], wd_ref[...], NT, preferred_element_type=F32)
 
     def pair_sum(g, v, lo, n):
         rows = at(v * YR + lo, n, 64)
@@ -270,7 +267,7 @@
     lo, hi = pl.ds(0, YR // 2), pl.ds(YR // 2, YR // 2)
 
     def gh_rows(g, y_, start, n):
-        return gh.at[at(g * 2 * HALF + k * HALF + y_ * YR + start, n, HR)]
+        return gh.at[at(g * 2 * HALF + k * HALF + y_ * YR + start, n, 16)]
 
     def summed(g):
         t = str(g)
@@ -288,52 +285,77 @@
         @task("Y" + t)
         def _():
             arrived(*made["P" + t])
-            y_out[g, 0] = pair_sum(g, y_far, 0, YR).astype(BF16)
-            a = send(y_out.at[g, 0, lo], y_mid.at[g, 0], y_right)
-            b = send(y_out.at[g, 0, hi], y_mid.at[g, 1], y_left)
-            y_out[g, 1, hi] = pair_sum(g, y_next, YR // 2, YR // 2).astype(BF16)
+            y_out[g, 0] = pair_sum(g, y_far, 0, YR).astype(Y_TYPE)
+            if Y_DIRECT:
+                a = send(y_out.at[g, 0], y_in.at[g, 2], y_over)
+                y_out[g, 1] = pair_sum(g, y_next, 0, YR).astype(Y_TYPE)
+                b = send(y_out.at[g, 1], y_in.at[g, 0], y_right)
+                y_out[g, 2] = pair_sum(g, y_prev, 0, YR).astype(Y_TYPE)
+                return a, b, send(y_out.at[g, 2], y_in.at[g, 1], y_left)
+            a = send(y_out.at[g, 0, lo], y_in.at[g, 2, lo], y_right)
+            b = send(y_out.at[g, 0, hi], y_in.at[g, 2, hi], y_left)
+            y_out[g, 1, hi] = pair_sum(g, y_next, YR // 2, YR // 2).astype(Y_TYPE)
             c = send(y_out.at[g, 1, hi], y_in.at[g, 0, hi], y_right)
-            y_out[g, 2, lo] = pair_sum(g, y_prev, 0, YR // 2).astype(BF16)
+            y_out[g, 2, lo] = pair_sum(g, y_prev, 0, YR // 2).astype(Y_TYPE)
             d = send(y_out.at[g, 2, lo], y_in.at[g, 1, lo], y_left)
             return a, b, c, d
 
         @task("Z" + t)
         def _():
+            h_sum[g] = pair_sum(g, y, 0, YR)
+            if Y_DIRECT:
+                return made["Y" + t]
             a, b, c, d = made["Y" + t]
             arrived(a)
-            y_out[g, 1, lo] = (pair_sum(g, y_next, 0, YR // 2) + y_mid[g, 0].astype(F32)).astype(BF16)
+            y_out[g, 1, lo] = (pair_sum(g, y_next, 0, YR // 2) + y_in[g, 2, lo].astype(F32)).astype(Y_TYPE)
             e = send(y_out.at[g, 1, lo], y_in.at[g, 0, lo], y_right)
             arrived(b)
-            y_out[g, 2, hi] = (pair_sum(g, y_prev, YR // 2, YR // 2) + y_mid[g, 1].astype(F32)).astype(BF16)
+            y_out[g, 2, hi] = (pair_sum(g, y_prev, YR // 2, YR // 2) + y_in[g, 2, hi].astype(F32)).astype(Y_TYPE)
             f = send(y_out.at[g, 2, hi], y_in.at[g, 1, hi], y_left)
-            h_sum[g] = pair_sum(g, y, 0, YR)
             return c, d, e, f
 
         @task("H" + t)
         def _():
             arrived(*made["Z" + t])
-            h_sum[g] = h_sum[g] + y_in[g, 0].astype(F32) + y_in[g, 1].astype(F32)
-
-            def piece(v):
-                return h_sum.at[g, at(v * HR, HR, HR)]
+            total = h_sum[g] + y_in[g, 0].astype(F32) + y_in[g, 1].astype(F32)
+            h_sum[g] = total + y_in[g, 2].astype(F32) if Y_DIRECT else total
+
+            def piece(n, v):
+                h_out[g, n] = h_sum[g, at(v * HR, HR, HR)].astype(H_TYPE)
+                return h_out.at[g, n]
 
             return (
-                send(piece(h_far), h_in.at[g, 2], h_over),
-                send(piece(h_next), h_in.at[g, 0], h_right),
-                send(piece(h_prev), h_in.at[g, 1], h_left),
+                send(piece(0, h_far), h_in.at[g, 2], h_over),
+                send(piece(1, h_next), h_in.at[g, 0], h_right),
+                send(piece(2, h_prev), h_in.at[g, 1], h_left),
             )
 
         @task("I" + t)
         def _():
             arrived(*made["H" + t])
-            total = h_sum[g, at(h * HR, HR, HR)] + h_in[g, 0] + h_in[g, 1] + h_in[g, 2]
+            total = h_sum[g, at(h * HR, HR, HR)]
+            for n in range(3):
+                total = total + h_in[g, n].astype(F32)
             ref = gh_rows(g, y, h * HR, HR)
             ref[...] = total.astype(BF16)
-            return tuple(send(ref, ref, to) for to in (h_over, h_right, h_left))
+            tos = (h_right, h_left) if RING_OUT else (h_over, h_right, h_left)
+            return tuple(send(ref, ref, to) for to in tos)
+
+        @task("F" + t)
+        def _():
+            if not RING_OUT:
+                return made["I" + t]
+            a, b = made["I" + t]
+            arrived(a)
+            ref = gh_rows(g, y, h_prev * HR, HR // 2)
+            c = send(ref, ref, h_right)
+            arrived(b)
+            ref = gh_rows(g, y, h_next * HR + HR // 2, HR // 2)
+            return a, b, c, send(ref, ref, h_left)
 
         @task("J" + t)
         def _():
-            arrived(*made["I" + t])
+            arrived(*made["F" + t])
             ref = gh_rows(g, y, 0, YR)
             return tuple(send(ref, ref, to) for to in (y_right, y_left, twin))
 
@@ -362,7 +384,7 @@
         @task("R" + t)
         def _():
             arrived(*made["L" + t])
-            for name in ("I", "J", "K", "L"):
+            for name in ("I", "F", "J", "K", "L"):
                 gone(*made[name + t])
             for name in ACTS:
                 arrived(*made[name])
@@ -375,84 +397,134 @@
         other, steps = ORDER[place]
         return lax.rem(z + other, 2) * 4 + lax.rem(x + steps, 4)
 
-    def gradients(place, half):
+    def gradients(place):
         block = block_of(place)
 
-        @pl.loop(half * 16, half * 16 + 16, unroll=2)
+        @pl.loop(0, 8)
         def _(i):
-            pair = block * 2 + i // 16
-            core = lax.rem(i // 8, 2)
-            rows = at(lax.rem(i, 8) * 16, 16, 16)
-            flat = at(place * B + i * 16, 16, 16)
+            pair = block * 2 + i // 4
+            core = lax.rem(i // 2, 2)
+            rows = at(lax.rem(i, 2) * 64, 64, 64)
+            flat = at(place * B + i * 64, 64, 64)
             gate = act[0, pair, core, rows].astype(F32)
             up = act[1, pair, core, rows].astype(F32)
             grad = gh[flat].astype(F32)
-            sig = 0.5 * jnp.tanh(0.5 * gate) + 0.5
+            sig = jax.nn.sigmoid(gate)
             value = gate * sig
             act[0, pair, core, rows] = (value * up).astype(BF16)
             act[1, pair, core, rows] = (grad * up * sig * (1.0 + gate * (1.0 - sig))).astype(BF16)
             gh[flat] = (grad * value).astype(BF16)
 
-    def input_terms(place, half):
+    def input_terms(place, half=None):
         loaded(5)
         loaded(6)
-        grad_gate = act[1, block_of(place) * 2 + half].reshape(256, B)
-        grad_up = gh[pl.ds(place * B + half * 256, 256)]
+        block = block_of(place)
+        if half is None:
+            grad_gate = act[1, pl.ds(block * 2, 2)].reshape(B, B)
+            grad_up = gh[pl.ds(place * B, B)]
+        else:
+            grad_gate = act[1, block * 2 + half].reshape(B // 2, B)
+            grad_up = gh[pl.ds(place * B + half * (B // 2), B // 2)]
         gate_term = lax.dot_general(grad_gate, wg_ref[...], NT, preferred_element_type=F32)
         return gate_term + lax.dot_general(grad_up, wu_ref[...], NT, preferred_element_type=F32)
 
-    halves = ((0, "a", first), (1, "b", second))
+    def send_halves(n, to):
+        return tuple(send(x_out.at[n, rows], x_in.at[n, rows], to) for _, _, rows in halves)
 
     def out(name, n, where, to):
+        @task("u" + name)
+        def _():
+            gradients(AT[where])
+            x_out[n] = input_terms(AT[where]).astype(BF16)
+            return send_halves(n, to)
+
+    def ring(name, n, where, to, onward, source, m):
+        @task("v" + name)
+        def _():
+            gradients(AT[where])
+
         for half, t, rows in halves:
             def one(half=half, t=t, rows=rows):
                 @task("u" + name + t)
                 def _():
-                    gradients(AT[where], half)
-                    x_out[n, rows] = input_terms(AT[where], half).astype(BF16)
+                    total = input_terms(AT[where], half)
+                    if t == onward:
+                        arrived(made[source + t][0])
+                        total = total + x_in[m, rows].astype(F32)
+                    x_out[n, rows] = total.astype(BF16)
                     return (send(x_out.at[n, rows], x_in.at[n, rows], to),)
             one()
 
-    out("01", 0, (0, 1), x_right)
-    out("03", 1, (0, 3), x_left)
-    out("11", 3, (1, 1), x_right)
-    out("13", 4, (1, 3), x_left)
-    out("12", 2, (1, 2), z_pair)
+    if X_RING:
+        ring("01", 0, (0, 1), x_right, "a", "u02", 5)
+        ring("03", 1, (0, 3), x_left, "b", "u02", 5)
+    else:
+        out("01", 0, (0, 1), x_right)
+        out("03", 1, (0, 3), x_left)
+    if FAR_BY_X:
+        ring("11", 3, (1, 1), x_right, "a", "u12", 2)
+        ring("13", 4, (1, 3), x_left, "b", "u12", 2)
+    else:
+        out("11", 3, (1, 1), x_right)
+        out("13", 4, (1, 3), x_left)
+
+    @task("v12")
+    def _():
+        gradients(AT[1, 2])
+
+    @task("v02")
+    def _():
+        gradients(AT[0, 2])
+
+    @task("u00")
+    def _():
+        gradients(AT[0, 0])
+        acc[0] = input_terms(AT[0, 0])
+
+    @task("u10")
+    def _():
+        gradients(AT[1, 0])
+        acc[1] = input_terms(AT[1, 0])
 
     def rest(half, t, rows):
-        @task("v02" + t)
-        def _():
-            gradients(AT[0, 2], half)
-
         @task("u02" + t)
         def _():
-            arrived(*made["u12" + t])
-            total = input_terms(AT[0, 2], half) + x_in[2, rows].astype(F32)
+            total = input_terms(AT[0, 2], half)
+            if not FAR_BY_X:
+                arrived(*made["u12" + t])
+                total = total + x_in[2, rows].astype(F32)
             x_out[5, rows] = total.astype(BF16)
-            return (send(x_out.at[5, rows], x_in.at[5, rows], x_far),)
-
-        @task("u00" + t)
-        def _():
-            gradients(AT[0, 0], half)
-            acc[0, rows] = input_terms(AT[0, 0], half)
-
-        @task("u10" + t)
-        def _():
-            gradients(AT[1, 0], half)
-            acc[1, rows] = input_terms(AT[1, 0], half)
+            to = (x_right if t == "a" else x_left) if X_RING else x_far
+            return (send(x_out.at[5, rows], x_in.at[5, rows], to),)
+
+        @task("u12" + t)
+        def _():
+            x_out[2, rows] = input_terms(AT[1, 2], half).astype(BF16)
+            to = (x_right if t == "a" else x_left) if FAR_BY_X else z_pair
+            return (send(x_out.at[2, rows], x_in.at[2, rows], to),)
+
+        def sums_of(*names):
+            for name in names:
+                if name in made:
+                    arrived(made[name][half])
+                else:
+                    arrived(*made[name + t])
 
         @task("s1" + t)
         def _():
-            arrived(*made["u11" + t], *made["u13" + t])
+            sums_of("u11", "u13")
             total = acc[1, rows] + x_in[3, rows].astype(F32) + x_in[4, rows].astype(F32)
             x_out[6, rows] = total.astype(BF16)
             return (send(x_out.at[6, rows], x_in.at[6, rows], z_pair),)
 
         @task("s0" + t)
         def _():
-            arrived(*made["u01" + t], *made["u03" + t], *made["u02" + t], *made["s1" + t])
+            sums_of("u01", "u03", "s1")
             total = acc[0, rows]
-            for n in (0, 1, 5, 6):
+            if not X_RING:
+                sums_of("u02")
+                total = total + x_in[5, rows].astype(F32)
+            for n in (0, 1, 6):
                 total = total + x_in[n, rows].astype(F32)
             ig_ref[rows] = total.astype(BF16)
             return save(0, rows)
@@ -462,34 +534,30 @@
 
     def weight_grads(places, which, out_ref, last):
         scale = (8 * B) ** -0.5
-
-        @pl.loop(0, 2)
-        def _(i):
-            rows = at(i * 256, 256, 256)
-            total = None
-            for place in places:
-                block = block_of(place)
-                if which == 0:
-                    left = act[0, pl.ds(block * 2, 2), :, :, rows].reshape(B, 256)
-                    right = go[place]
+        total = None
+        for place in places:
+            block = block_of(place)
+            if which == 0:
+                left = act[0, pl.ds(block * 2, 2)].reshape(B, B)
+                right = go[place]
+            else:
+                left = inp[place]
+                if which == 1:
+                    right = act[1, pl.ds(block * 2, 2)].reshape(B, B)
                 else:
-                    left = inp[place, :, rows]
-                    if which == 1:
-                        right = act[1, pl.ds(block * 2, 2)].reshape(B, B)
-                    else:
-                        right = gh[pl.ds(place * B, B)]
-                term = lax.dot_general(left, right, TN, preferred_element_type=F32)
-                total = term if total is None else total + term
-            if last:
-                out_ref[rows] = ((total + held[which, rows]) * scale).astype(BF16)
-            else:
-                held[which, rows] = total
+                    right = gh[pl.ds(place * B, B)]
+            term = lax.dot_general(left, right, TN, preferred_element_type=F32)
+            total = term if total is None else total + term
+        if last:
+            out_ref[...] = ((total + held[which]) * scale).astype(BF16)
+        else:
+            held[which] = total
 
     def weights(name, which, out_ref):
         @task(name + "0")
         def _():
             if which:
-                for n in INS[:2]:
+                for n in INS[:4]:
                     arrived(*made[n])
             weight_grads((0, 1, 2, 3), which, out_ref, False)
 
@@ -545,17 +613,17 @@
             pltpu.VMEM((GROUPS, HALF, B), F32),
             pltpu.VMEM((GROUPS, HALF, B), F32),
             pltpu.VMEM((GROUPS, HALF, B), F32),
-            pltpu.VMEM((GROUPS, 3, YR, B), BF16),
-            pltpu.VMEM((GROUPS, 2, YR // 2, B), BF16),
-            pltpu.VMEM((GROUPS, 2, YR, B), BF16),
+            pltpu.VMEM((GROUPS, 3, YR, B), Y_TYPE),
+            pltpu.VMEM((GROUPS, 3, YR, B), Y_TYPE),
             pltpu.VMEM((GROUPS, YR, B), F32),
-            pltpu.VMEM((GROUPS, 3, HR, B), F32),
+            pltpu.VMEM((GROUPS, 3, HR, B), H_TYPE),
+            pltpu.VMEM((GROUPS, 3, HR, B), H_TYPE),
             pltpu.VMEM((7, B, B), BF16),
             pltpu.VMEM((7, B, B), BF16),
             pltpu.VMEM((2, B, B), F32),
             pltpu.VMEM((3, B, B), F32),
-            pltpu.SemaphoreType.DMA((160,)),
-            pltpu.SemaphoreType.DMA((160,)),
+            pltpu.SemaphoreType.DMA((200,)),
+            pltpu.SemaphoreType.DMA((200,)),
             pltpu.SemaphoreType.DMA((12,)),
         ],
         compiler_params=pltpu.CompilerParams(

time: 130 us -> 132 us (1.015)
  Pallas kernels: 129 us -> 131 us
    pallas_call x1, Pallas kernels: 127 us -> 129 us  [per_device(): pl.pallas_call(kernel, name='slab_backward', out_shape=(block,) * 4, in_s...]
where the time goes in v3:
time: 132 us
  Pallas kernels  131 us (99%)
    pallas_call x1, Pallas kernels, per_device(): pl.pallas_call(kernel, name='slab_backward', out_shape=(block,) * 4, in_s...  129 us

profile of v3, /device:TPU:1, one launch (start us, length us, event | category | flops | bytes accessed | tf_op | source)
XLA Modules:
  0.0 131.9 jit_solution(3515847461324589786)
XLA Ops:
  0.6 128.6 %slab_backward.1 = (bf16[512,512]{1,0:T(8,128)(2,1)}, bf16[512,512]{1,0:T(8,128)(2,1)}, bf16[512,512]{1,0:T(8,128)(2,1)}, bf16[512,512]{1,0:T(8,128)(2,1)}) custom-call(bf16[512,512]{1,0:T(8,128)(2,1)} %go_hbm.1, bf16[512,512]{1,0:T(8,128)(2,1)} %in_hbm.1, bf16[128,512]{1,0:T(8,128)(2,1)} %gate_hbm.1, bf16[128,512]{1,0:T(8,128)(2,1)} %up_hbm.1, ...), custom_call_target="tpu_custom_call" | custom-call | flops 12884901888 | bytes 3145728 | tf_op jit(solution)/shard_map/slab_backward/pallas_call | solution.py:600
  129.3 2.4 %hand_on.1 = (bf16[512,512]{1,0:T(8,128)(2,1)}, bf16[512,512]{1,0:T(8,128)(2,1)}, bf16[512,512]{1,0:T(8,128)(2,1)}, bf16[512,512]{1,0:T(8,128)(2,1)}) custom-call(bf16[512,512]{1,0:T(8,128)(2,1)} %get-tuple-element.8.refs_0_, bf16[512,512]{1,0:T(8,128)(2,1)} %get-tuple-element.9.refs_1_, bf16[512,512]{1,0:T(8,128)(2,1)} %get-tuple-element.10.refs_2_, ...), custom_call_target="tpu_custom_call" | custom-call | tf_op jit(solution)/shard_map/hand_on/pallas_call | solution.py:634

commit v4 on v3

--- a/solution.py
+++ b/solution.py
@@ -18,22 +18,23 @@
 YR = HALF // 4
 HR = YR // 4
 X_RING, FAR_BY_X = False, False
+SPLIT = False
 Y_DIRECT = False
 Y_TYPE, H_TYPE = BF16, BF16
 RING_IN, RING_OUT = False, False
 INS = ("in0a", "in0b", "in3a", "in3b", "in1a", "in1b", "in2a", "in2b", "in4a", "in4b")
 ACTS = ("a0", "a1", "a2", "a3", "bp", "bn", "bf", "cp", "cn", "cf", "t0", "t1", "t2")
 SCHEDULE = (
-    "go1b", "a1", "go0a", "go0b", "go1a", "a3", "go3b", "a0", "P3", "go3a",
-    "P0", "Y3", "Y0", "Z3", "in1b", "in1a", "go4b", "go2a", "Z0", "P1",
-    "go2b", "bp", "a2", "go4a", "Y1", "Z1", "in0b", "bn", "in0a", "P2",
-    "H1", "cp", "in3a", "Y2", "I1", "bf", "Z2", "H0", "in3b", "in2a",
-    "H3", "F1", "t0", "cn", "H2", "J1", "in4a", "in2b", "I0", "cf",
-    "t1", "I2", "F0", "K1", "J0", "F2", "t2", "I3", "L1", "in4b",
-    "J2", "R1", "u13", "K0", "u11", "F3", "K2", "L0", "R0", "u01",
-    "L2", "J3", "R2", "v12", "u12b", "u03", "K3", "d0", "u12a", "w0",
-    "L3", "R3", "u10", "s1b", "s1a", "v02", "u02b", "u00", "g0", "u02a",
-    "g1", "w1", "d1", "s0b", "s0a",
+    "go1a", "a1", "go0a", "go3a", "a0", "go0b", "go1b", "a3", "go3b", "P3",
+    "P0", "Y3", "Y0", "Z3", "in1a", "Z0", "P1", "bn", "go2b", "in1b",
+    "a2", "go4a", "go4b", "go2a", "Y1", "bp", "Z1", "in0a", "H0", "bf",
+    "P2", "H1", "t0", "in0b", "Y2", "H3", "in3a", "I1", "cn", "I3",
+    "Z2", "I0", "F3", "F1", "J1", "H2", "cp", "in2a", "cf", "F0",
+    "t1", "in2b", "K1", "I2", "in3b", "J0", "in4a", "L1", "in4b", "t2",
+    "J3", "F2", "K0", "J2", "R1", "u13", "u11", "L0", "K2", "R0",
+    "u01", "K3", "L2", "R2", "v12", "u12a", "L3", "u03", "R3", "u10",
+    "u12b", "u00", "v02", "w0", "s1a", "u02a", "w1", "u02b", "s1b", "d0",
+    "g0", "g1", "d1", "s0a", "s0b",
 )
 NT = (((1,), (1,)), ((), ()))
 TN = (((0,), (0,)), ((), ()))
@@ -149,10 +150,12 @@
         paired = buf.at[AT[1, 0]]
 
         def one(half, t, rows):
+            part_of = rows if SPLIT else pl.ds(0, B)
+
             def both_ways(src, plane):
                 return (
-                    send(src, buf.at[AT[plane, 3], rows], x_right),
-                    send(src, buf.at[AT[plane, 1], rows], x_left),
+                    send(src, buf.at[AT[plane, 3], part_of], x_right),
+                    send(src, buf.at[AT[plane, 1], part_of], x_left),
                 )
 
             def far(plane):
@@ -163,12 +166,16 @@
             @task(name + "0" + t)
             def _():
                 loaded(load)
-                return both_ways(mine.at[rows], 0)
+                if half == 1 and not SPLIT:
+                    return made[name + "0a"]
+                return both_ways(mine.at[part_of], 0)
 
             @task(name + "1" + t)
             def _():
                 loaded(load)
-                return (send(mine.at[rows], buf.at[AT[1, 0], rows], z_pair),)
+                if half == 1 and not SPLIT:
+                    return made[name + "1a"]
+                return (send(mine.at[part_of], buf.at[AT[1, 0], part_of], z_pair),)
 
             @task(name + "2" + t)
             def _():
@@ -178,7 +185,9 @@
             @task(name + "3" + t)
             def _():
                 arrived(*made[name + "1" + t])
-                return both_ways(paired.at[rows], 1)
+                if half == 1 and not SPLIT:
+                    return made[name + "3a"]
+                return both_ways(paired.at[part_of], 1)
 
             @task(name + "4" + t)
             def _():

time: 132 us -> 129 us (0.977)
  Pallas kernels: 131 us -> 128 us
    pallas_call x1, Pallas kernels: 129 us -> 125 us  [per_device(): pl.pallas_call(kernel, name='slab_backward', out_shape=(block,) * 4, in_s...]
where the time goes in v4:
time: 129 us; the launch traced here: 128 us
  Pallas kernels  128 us (99%)
    pallas_call x1, Pallas kernels, per_device(): pl.pallas_call(kernel, name='slab_backward', out_shape=(block,) * 4, in_s...  125 us

profile of v4, /device:TPU:1, one launch (start us, length us, event | category | flops | bytes accessed | tf_op | source)
XLA Modules:
  0.0 128.4 jit_solution(16818392282852249412)
XLA Ops:
  0.6 125.2 %slab_backward.1 = (bf16[512,512]{1,0:T(8,128)(2,1)}, bf16[512,512]{1,0:T(8,128)(2,1)}, bf16[512,512]{1,0:T(8,128)(2,1)}, bf16[512,512]{1,0:T(8,128)(2,1)}) custom-call(bf16[512,512]{1,0:T(8,128)(2,1)} %go_hbm.1, bf16[512,512]{1,0:T(8,128)(2,1)} %in_hbm.1, bf16[128,512]{1,0:T(8,128)(2,1)} %gate_hbm.1, bf16[128,512]{1,0:T(8,128)(2,1)} %up_hbm.1, ...), custom_call_target="tpu_custom_call" | custom-call | flops 12884901888 | bytes 3145728 | tf_op jit(solution)/shard_map/slab_backward/pallas_call | solution.py:609
  125.8 2.4 %hand_on.1 = (bf16[512,512]{1,0:T(8,128)(2,1)}, bf16[512,512]{1,0:T(8,128)(2,1)}, bf16[512,512]{1,0:T(8,128)(2,1)}, bf16[512,512]{1,0:T(8,128)(2,1)}) custom-call(bf16[512,512]{1,0:T(8,128)(2,1)} %get-tuple-element.8.refs_0_, bf16[512,512]{1,0:T(8,128)(2,1)} %get-tuple-element.9.refs_1_, bf16[512,512]{1,0:T(8,128)(2,1)} %get-tuple-element.10.refs_2_, ...), custom_call_target="tpu_custom_call" | custom-call | tf_op jit(solution)/shard_map/hand_on/pallas_call | solution.py:643

commit v5 on v4

--- a/solution.py
+++ b/solution.py
@@ -25,16 +25,16 @@
 INS = ("in0a", "in0b", "in3a", "in3b", "in1a", "in1b", "in2a", "in2b", "in4a", "in4b")
 ACTS = ("a0", "a1", "a2", "a3", "bp", "bn", "bf", "cp", "cn", "cf", "t0", "t1", "t2")
 SCHEDULE = (
-    "go1a", "a1", "go0a", "go3a", "a0", "go0b", "go1b", "a3", "go3b", "P3",
-    "P0", "Y3", "Y0", "Z3", "in1a", "Z0", "P1", "bn", "go2b", "in1b",
-    "a2", "go4a", "go4b", "go2a", "Y1", "bp", "Z1", "in0a", "H0", "bf",
-    "P2", "H1", "t0", "in0b", "Y2", "H3", "in3a", "I1", "cn", "I3",
-    "Z2", "I0", "F3", "F1", "J1", "H2", "cp", "in2a", "cf", "F0",
-    "t1", "in2b", "K1", "I2", "in3b", "J0", "in4a", "L1", "in4b", "t2",
-    "J3", "F2", "K0", "J2", "R1", "u13", "u11", "L0", "K2", "R0",
-    "u01", "K3", "L2", "R2", "v12", "u12a", "L3", "u03", "R3", "u10",
-    "u12b", "u00", "v02", "w0", "s1a", "u02a", "w1", "u02b", "s1b", "d0",
-    "g0", "g1", "d1", "s0a", "s0b",
+    "go1a", "a1", "go0a", "go3a", "go1b", "a0", "a3", "go0b", "P0", "P3",
+    "Y0", "go3b", "Y3", "Z0", "go2a", "in1a", "go2b", "Z3", "go4a", "go4b",
+    "P1", "bp", "a2", "Y1", "in1b", "bn", "Z1", "in0a", "P2", "H0",
+    "Y2", "H1", "bf", "in0b", "in3a", "I0", "cn", "Z2", "I1", "cp",
+    "H2", "in2a", "F1", "J1", "t0", "t1", "in3b", "H3", "cf", "in4b",
+    "F0", "I2", "in2b", "F2", "K1", "in4a", "J0", "t2", "L1", "I3",
+    "J2", "R1", "u13", "K0", "u11", "K2", "L0", "R0", "u03", "L2",
+    "F3", "J3", "R2", "v12", "u12a", "u01", "K3", "u12b", "w0", "g0",
+    "L3", "v02", "R3", "u10", "s1a", "u02a", "s1b", "u02b", "u00", "g1",
+    "d0", "d1", "w1", "s0a", "s0b",
 )
 NT = (((1,), (1,)), ((), ()))
 TN = (((0,), (0,)), ((), ()))

time: 129 us -> 127 us (0.984)
  Pallas kernels: 128 us -> 126 us
    pallas_call x1, Pallas kernels: 125 us -> 124 us  [per_device(): pl.pallas_call(kernel, name='slab_backward', out_shape=(block,) * 4, in_s...]
where the time goes in v5:
time: 127 us
  Pallas kernels  126 us (99%)
    pallas_call x1, Pallas kernels, per_device(): pl.pallas_call(kernel, name='slab_backward', out_shape=(block,) * 4, in_s...  124 us

profile of v5, /device:TPU:1, one launch (start us, length us, event | category | flops | bytes accessed | tf_op | source)
XLA Modules:
  0.0 127.1 jit_solution(5183307755392363958)
XLA Ops:
  0.6 123.9 %slab_backward.1 = (bf16[512,512]{1,0:T(8,128)(2,1)}, bf16[512,512]{1,0:T(8,128)(2,1)}, bf16[512,512]{1,0:T(8,128)(2,1)}, bf16[512,512]{1,0:T(8,128)(2,1)}) custom-call(bf16[512,512]{1,0:T(8,128)(2,1)} %go_hbm.1, bf16[512,512]{1,0:T(8,128)(2,1)} %in_hbm.1, bf16[128,512]{1,0:T(8,128)(2,1)} %gate_hbm.1, bf16[128,512]{1,0:T(8,128)(2,1)} %up_hbm.1, ...), custom_call_target="tpu_custom_call" | custom-call | flops 12884901888 | bytes 3145728 | tf_op jit(solution)/shard_map/slab_backward/pallas_call | solution.py:609
  124.5 2.4 %hand_on.1 = (bf16[512,512]{1,0:T(8,128)(2,1)}, bf16[512,512]{1,0:T(8,128)(2,1)}, bf16[512,512]{1,0:T(8,128)(2,1)}, bf16[512,512]{1,0:T(8,128)(2,1)}) custom-call(bf16[512,512]{1,0:T(8,128)(2,1)} %get-tuple-element.8.refs_0_, bf16[512,512]{1,0:T(8,128)(2,1)} %get-tuple-element.9.refs_1_, bf16[512,512]{1,0:T(8,128)(2,1)} %get-tuple-element.10.refs_2_, ...), custom_call_target="tpu_custom_call" | custom-call | tf_op jit(solution)/shard_map/hand_on/pallas_call | solution.py:643
